TPU v7x, 128 devices: a whole 4x4x4 slice. The times are simulated.
128 devices in a mesh: frame: 16 (over x, y_lo, core), dp: 8 (over z, y_hi).
Axes of the slice: x: 4, y: 4 (y_hi: 2, y_lo: 2; y = y_hi * 2 + y_lo), z: 4, core: 2. Of those that a mesh axis runs over, the one named last changes fastest.
Arguments:
- tokens: bfloat16 [6144, 5120], P(('frame', 'dp')), may hold values from -8 to 8
- qkv_weight: bfloat16 [5120, 3, 3072], P(None, None, 'dp'), may hold values from -0.078125 to 0.078125
- out_weight: bfloat16 [3072, 5120], P('dp'), may hold values from -0.109375 to 0.109375
- mod_table: float32 [8, 3, 5120], replicated, may hold values from -3 to 3
- levels: int32 [16], replicated, may hold values from 0 to 6
- frame_order: int32 [16], replicated, may hold values from 0 to 15, each once
Outputs:
- hidden: bfloat16 [6144, 5120], P(('frame', 'dp'))
- attended: bfloat16 [6144, 3072], P('frame', 'dp')
Inputs may be any that keep to these rules, and one draw needn't show every extreme that they name: levels + 1 is a row of mod_table. frame_order names each place in time once.
All inputs are finite; a program needn't handle non-finite values.
Results may differ from a plain program's by a relative error of at most 0.012.
Values may be sent and summed in bfloat16 or wider, within the bound.
No kernel may reach another device: no remote copies, remote signals or barrier semaphores. Data moves between devices by JAX's collectives and lax.ppermute only.
A program may use at most 192 MiB of HBM per device.

v0:
```python
import math

import jax
import jax.numpy as jnp
from jax import lax
from jax.sharding import PartitionSpec as P

HEAD = 128
STEPS = 2


EPSILON = 1e-06


def layer_normed(values):
    average = jnp.mean(values, axis=-1, keepdims=True)
    centered = values - average
    variance = jnp.mean(centered * centered, axis=-1, keepdims=True)
    return centered * lax.rsqrt(variance + EPSILON)


def head_normed(values):
    return values * lax.rsqrt(jnp.mean(values * values, axis=-1, keepdims=True) + EPSILON)


def modulated(hidden, mod_row):
    return (layer_normed(hidden.astype(jnp.float32)) * (1.0 + mod_row[1]) + mod_row[0]).astype(
        jnp.bfloat16
    )


def per_device(tokens, qkv_weight, out_weight, mod_table, levels, frame_order):
    own_rows = tokens.shape[0]
    model_width = tokens.shape[1]
    group_count = lax.axis_size("dp")
    frame_rows = own_rows * group_count
    inner_dev = qkv_weight.shape[2]
    heads_dev = inner_dev // HEAD
    frame_total = frame_order.shape[0]
    frame_index = lax.axis_index("frame")
    frame_ids = jnp.arange(frame_total, dtype=jnp.int32)
    own_rank = jnp.sum(jnp.where(frame_ids == frame_index, frame_order, 0))
    own_level = jnp.sum(jnp.where(frame_ids == frame_index, levels, 0))
    weights_flat = qkv_weight.reshape(model_width, 3 * inner_dev)
    factor = 1.0 / math.sqrt(HEAD)
    level_ids = jnp.arange(mod_table.shape[0], dtype=jnp.int32)
    hidden = tokens
    attended = None
    for step_index in range(STEPS):
        picked = level_ids == own_level + step_index
        mod_row = jnp.sum(jnp.where(picked[:, None, None], mod_table, 0.0), axis=0)
        normed = modulated(hidden, mod_row)
        projected = jnp.dot(
            lax.all_gather(normed, "dp", axis=0, tiled=True),
            weights_flat,
            preferred_element_type=jnp.float32,
        )
        queries = head_normed(projected[:, :inner_dev].reshape(frame_rows, heads_dev, HEAD)).astype(
            jnp.bfloat16
        )
        key_rows = head_normed(
            projected[:, inner_dev : 2 * inner_dev].reshape(frame_rows, heads_dev, HEAD)
        )
        key_rows = key_rows.astype(jnp.bfloat16).reshape(frame_rows, inner_dev)
        value_rows = projected[:, 2 * inner_dev :].astype(jnp.bfloat16)
        key_piece = lax.all_gather(key_rows, "frame", axis=0, tiled=True)
        value_piece = lax.all_gather(value_rows, "frame", axis=0, tiled=True)
        key_count = key_piece.shape[0]
        key_frames = jnp.arange(key_count, dtype=jnp.int32) // frame_rows
        key_ranks = jnp.sum(
            jnp.where(key_frames[:, None] == frame_ids[None, :], frame_order[None, :], 0), axis=1
        )
        visible = key_ranks <= own_rank
        scores = (
            jnp.einsum(
                "qhd,khd->hqk",
                queries,
                key_piece.reshape(key_count, heads_dev, HEAD),
                preferred_element_type=jnp.float32,
            )
            * factor
        )
        weights = jnp.where(visible[None, None, :], jnp.exp(scores), 0.0)
        denominator = jnp.sum(weights, axis=-1)
        numerator = jnp.einsum(
            "hqk,khd->qhd",
            weights.astype(jnp.bfloat16),
            value_piece.reshape(key_count, heads_dev, HEAD),
            preferred_element_type=jnp.float32,
        )
        numerator, denominator = (numerator, denominator)
        mixture = numerator / jnp.transpose(denominator)[:, :, None]
        attended = mixture.astype(jnp.bfloat16).reshape(frame_rows, inner_dev)
        branch = lax.psum_scatter(
            jnp.dot(attended, out_weight, preferred_element_type=jnp.float32).astype(jnp.bfloat16),
            "dp",
            scatter_dimension=0,
            tiled=True,
        ).astype(jnp.float32)
        hidden = (hidden.astype(jnp.float32) + mod_row[2] * branch).astype(jnp.bfloat16)
    return (hidden, attended)


def solution(mesh):
    return jax.shard_map(
        per_device,
        mesh=mesh,
        in_specs=(P(("frame", "dp"), None), P(None, None, "dp"), P("dp", None), P(), P(), P()),
        out_specs=(P(("frame", "dp"), None), P("frame", "dp")),
        check_vma=False,
    )
```

profile of v0, /device:TPU:0, one launch (start us, length us, event | category | flops | bytes accessed | tf_op | source)
XLA Modules:
  0.0 559.1 jit_solution(5347292020685369262)
XLA Ops:
  7.2 1.3 fusion.53
  9.8 1.2 convert_reduce_fusion.1
  11.0 1.3 fusion.40
  12.4 1.4 select_reduce_fusion
  13.9 2.1 fusion.43
  16.1 16.0 %copy.33 = bf16[5120,3,384]{0,2,1:T(8,128)(2,1)} copy(bf16[5120,3,384]{2,0,1:T(8,128)(2,1)} %param.7) | data formatting | bytes 23592960 | tf_op args[1]
  32.0 56.0 %all-gather.7.cloned.1.call-done = bf16[384,5120]{1,0:T(8,128)(2,1)} async-done(((bf16[48,5120]{1,0:T(8,128)(2,1)}), bf16[384,5120]{1,0:T(8,128)(2,1)}) %all-gather.7.cloned.1.call-update) | async-done | bytes 3932176 | tf_op jit(solution)/shard_map/all_gather | solution.py:54
  88.0 10.0 %fusion.64 = f32[384,1152]{1,0:T(8,128)S(1)} fusion(bf16[384,5120]{1,0:T(8,128)(2,1)} %all-gather.7.cloned.1.call-done, bf16[5120,1152]{0,1:T(8,128)(2,1)} %bitcast.45), kind=kOutput, calls=%fused_computation.92 | convolution fusion | flops 4529848320 | bytes 17498112 | tf_op jit(solution)/shard_map/dot_general | solution.py:53
  98.7 0.8 fusion.61
  102.0 33.7 %all-gather.11.cloned.1.call-done = bf16[6144,384]{1,0:T(8,128)(2,1)} async-done(((bf16[384,384]{1,0:T(8,128)(2,1)}), bf16[6144,384]{1,0:T(8,128)(2,1)}) %all-gather.11.cloned.1.call-update) | async-done | bytes 4718608 | tf_op jit(solution)/shard_map/all_gather | solution.py:66
  135.8 6.7 %copy.38 = bf16[6144,384]{0,1:T(8,128)(2,1)} copy(bf16[6144,384]{1,0:T(8,128)(2,1)} %all-gather.11.cloned.1.call-done) | data formatting | bytes 9437184 | tf_op jit(solution)/shard_map/all_gather | solution.py:66
  142.4 15.1 %fusion = (f32[3,384]{1,0:T(4,128)S(1)}, f32[3,384,6144]{2,1,0:T(8,128)}) fusion(pred[6144]{0:T(1024)(128)(4,1)S(1)} %broadcast_compare_fusion, bf16[6144,3,128]{0,2,1:T(8,128)(2,1)} %bitcast.47, f32[384,3,128]{0,2,1:T(8,128)S(1)} %bitcast.52, f32[384,3]{0,1:T(4,128)S(1)} %add_rsqrt_fusion.3), kind=kOutput, calls=%fused_computation.2 | convolution fusion | flops 1833466752 | bytes 33635328 | tf_op jit(solution)/shard_map/qhd,khd->hqk/dot_general | solution.py:75
  157.5 19.0 %all-gather.9.cloned.1.call-done = bf16[6144,384]{1,0:T(8,128)(2,1)} async-done(((bf16[384,384]{1,0:T(8,128)(2,1)}), bf16[6144,384]{1,0:T(8,128)(2,1)}) %all-gather.9.cloned.1.call-update) | async-done | bytes 4718608 | tf_op jit(solution)/shard_map/all_gather | solution.py:67
  176.5 6.7 %copy.34 = bf16[6144,384]{0,1:T(8,128)(2,1)} copy(bf16[6144,384]{1,0:T(8,128)(2,1)} %all-gather.9.cloned.1.call-done) | data formatting | bytes 9437184 | tf_op jit(solution)/shard_map/all_gather | solution.py:67
  183.1 12.8 %fusion.33 = bf16[384,3,128]{0,2,1:T(8,128)(2,1)S(1)} fusion(bf16[6144,3,128]{0,2,1:T(8,128)(2,1)} %bitcast.50, f32[3,384,6144]{2,1,0:T(8,128)} %get-tuple-element.23, pred[6144]{0:T(1024)(128)(4,1)S(1)} %broadcast_compare_fusion, f32[384,3]{0,1:T(4,128)S(1)} %bitcast.69), kind=kOutput, calls=%fused_computation.31 | convolution fusion | flops 1833467904 | bytes 33335808 | tf_op jit(solution)/shard_map/hqk,khd->qhd/dot_general | solution.py:85
  196.0 4.1 convolution_convert_fusion.1
  200.4 83.2 %reduce-scatter.3.cloned.1.call-done = bf16[48,5120]{1,0:T(8,128)(2,1)} async-done(((bf16[384,5120]{1,0:T(8,128)(2,1)}), bf16[48,5120]{1,0:T(8,128)(2,1)}) %reduce-scatter.3.cloned.1.call-update) | async-done | bytes 491536 | tf_op jit(solution)/shard_map/reduce_scatter | solution.py:94
  283.7 1.3 convert_reduce_fusion
  285.3 1.0 fusion.39
  286.4 68.4 %all-gather.13.cloned.1.call-done = bf16[384,5120]{1,0:T(8,128)(2,1)} async-done(((bf16[48,5120]{1,0:T(8,128)(2,1)}), bf16[384,5120]{1,0:T(8,128)(2,1)}) %all-gather.13.cloned.1.call-update) | async-done | bytes 3932176 | tf_op jit(solution)/shard_map/all_gather | solution.py:54
  354.8 10.0 %fusion.65 = f32[384,1152]{1,0:T(8,128)S(1)} fusion(bf16[384,5120]{1,0:T(8,128)(2,1)} %all-gather.13.cloned.1.call-done, bf16[5120,1152]{0,1:T(8,128)(2,1)} %bitcast.46), kind=kOutput, calls=%fused_computation.93 | convolution fusion | flops 4529848320 | bytes 17498112 | tf_op jit(solution)/shard_map/dot_general | solution.py:53
  365.4 0.8 fusion.60
  367.4 35.1 %all-gather.17.cloned.1.call-done = bf16[6144,384]{1,0:T(8,128)(2,1)} async-done(((bf16[384,384]{1,0:T(8,128)(2,1)}), bf16[6144,384]{1,0:T(8,128)(2,1)}) %all-gather.17.cloned.1.call-update) | async-done | bytes 4718608 | tf_op jit(solution)/shard_map/all_gather | solution.py:66
  402.5 6.7 %copy.45 = bf16[6144,384]{0,1:T(8,128)(2,1)} copy(bf16[6144,384]{1,0:T(8,128)(2,1)} %all-gather.17.cloned.1.call-done) | data formatting | bytes 9437184 | tf_op jit(solution)/shard_map/all_gather | solution.py:66
  409.2 15.1 %fusion.2 = (f32[3,384]{1,0:T(4,128)S(1)}, f32[3,384,6144]{2,1,0:T(8,128)}) fusion(pred[6144]{0:T(1024)(128)(4,1)S(1)} %broadcast_compare_fusion, bf16[6144,3,128]{0,2,1:T(8,128)(2,1)} %bitcast.48, f32[384,3,128]{0,2,1:T(8,128)S(1)} %bitcast.54, f32[384,3]{0,1:T(4,128)S(1)} %add_rsqrt_fusion.1), kind=kOutput, calls=%fused_computation.4 | convolution fusion | flops 1833466752 | bytes 33635328 | tf_op jit(solution)/shard_map/qhd,khd->hqk/dot_general | solution.py:75
  424.2 19.0 %all-gather.15.cloned.1.call-done = bf16[6144,384]{1,0:T(8,128)(2,1)} async-done(((bf16[384,384]{1,0:T(8,128)(2,1)}), bf16[6144,384]{1,0:T(8,128)(2,1)}) %all-gather.15.cloned.1.call-update) | async-done | bytes 4718608 | tf_op jit(solution)/shard_map/all_gather | solution.py:67
  443.2 6.7 %copy.41 = bf16[6144,384]{0,1:T(8,128)(2,1)} copy(bf16[6144,384]{1,0:T(8,128)(2,1)} %all-gather.15.cloned.1.call-done) | data formatting | bytes 9437184 | tf_op jit(solution)/shard_map/all_gather | solution.py:67
  449.9 12.8 %fusion.27 = bf16[384,3,128]{0,2,1:T(8,128)(2,1)S(1)} fusion(bf16[6144,3,128]{0,2,1:T(8,128)(2,1)} %bitcast.49, f32[3,384,6144]{2,1,0:T(8,128)} %get-tuple-element.25, pred[6144]{0:T(1024)(128)(4,1)S(1)} %broadcast_compare_fusion, f32[384,3]{0,1:T(4,128)S(1)} %bitcast.68), kind=kOutput, calls=%fused_computation.29 | convolution fusion | flops 1833467904 | bytes 33335808 | tf_op jit(solution)/shard_map/hqk,khd->qhd/dot_general | solution.py:85
  462.8 4.2 convolution_convert_fusion
  466.9 0.9 copy.48
  467.8 82.5 %reduce-scatter.5.cloned.1.call-done = bf16[48,5120]{1,0:T(8,128)(2,1)} async-done(((bf16[384,5120]{1,0:T(8,128)(2,1)}), bf16[48,5120]{1,0:T(8,128)(2,1)}) %reduce-scatter.5.cloned.1.call-update) | async-done | bytes 491536 | tf_op jit(solution)/shard_map/reduce_scatter | solution.py:94
  550.3 2.0 fusion.45
  (56 shorter events, 6.4 us)
Async XLA Ops:
  7.2 80.9 %all-gather.7.cloned.1.call-start = ((), (), s32[]{:S(2)}) async-start(), calls=%async_computation.2 | async-start | bytes 4423680 | tf_op jit(solution)/shard_map/all_gather | solution.py:54
  16.0 119.8 %all-gather.11.cloned.1.call-start = ((), (), s32[]{:S(2)}) async-start(), calls=%async_computation.4 | async-start | bytes 5013504 | tf_op jit(solution)/shard_map/all_gather | solution.py:66
  98.0 2.3 copy-start.3
  99.5 77.0 %all-gather.9.cloned.1.call-start = ((), (), s32[]{:S(2)}) async-start(), calls=%async_computation.3 | async-start | bytes 5013504 | tf_op jit(solution)/shard_map/all_gather | solution.py:67
  100.3 183.3 %reduce-scatter.3.cloned.1.call-start = ((), (), s32[]{:S(2)}) async-start(), calls=%async_computation.5 | async-start | bytes 4423680 | tf_op jit(solution)/shard_map/reduce_scatter | solution.py:94
  183.1 12.9 %copy-start = (bf16[384,5120]{1,0:T(8,128)(2,1)S(1)}, bf16[384,5120]{1,0:T(8,128)(2,1)}, u32[]{:S(2)}) copy-start(bf16[384,5120]{1,0:T(8,128)(2,1)} %param.8) | copy-start | bytes 11796484
  196.0 87.6 %copy-start.2 = (bf16[48,5120]{1,0:T(8,128)(2,1)S(1)}, bf16[48,5120]{1,0:T(8,128)(2,1)}, u32[]{:S(2)}) copy-start(bf16[48,5120]{1,0:T(8,128)(2,1)} %param.6) | copy-start | bytes 1474564
  200.2 154.6 %all-gather.13.cloned.1.call-start = ((), (), s32[]{:S(2)}) async-start(), calls=%async_computation.6 | async-start | bytes 4423680 | tf_op jit(solution)/shard_map/all_gather | solution.py:54
  286.4 116.2 %all-gather.17.cloned.1.call-start = ((), (), s32[]{:S(2)}) async-start(), calls=%async_computation.8 | async-start | bytes 5013504 | tf_op jit(solution)/shard_map/all_gather | solution.py:66
  366.3 77.0 %all-gather.15.cloned.1.call-start = ((), (), s32[]{:S(2)}) async-start(), calls=%async_computation.7 | async-start | bytes 5013504 | tf_op jit(solution)/shard_map/all_gather | solution.py:67
  367.1 183.3 %reduce-scatter.5.cloned.1.call-start = ((), (), s32[]{:S(2)}) async-start(), calls=%async_computation.9 | async-start | bytes 4423680 | tf_op jit(solution)/shard_map/reduce_scatter | solution.py:94
  449.9 12.9 %copy-start.1 = (bf16[384,5120]{1,0:T(8,128)(2,1)S(1)}, bf16[384,5120]{1,0:T(8,128)(2,1)}, u32[]{:S(2)}) copy-start(bf16[384,5120]{1,0:T(8,128)(2,1)} %param.8) | copy-start | bytes 11796484
Sparse Core Ops, SparseCore 0:
  16.1 71.8 all-gather.6
  99.6 36.0 all-gather.10
  138.1 38.3 all-gather.8
  200.3 83.2 reduce-scatter.2
  286.6 68.1 all-gather.12
  366.4 36.0 all-gather.16
  404.9 38.2 all-gather.14
  467.1 83.2 reduce-scatter.4
where the time goes:
time: 561 us; the launch traced here: 559 us
  waiting for transfers between devices  397 us (71%)
  matrix products  84.1 us (15%)
  local copies, waits for them, and re-layouts  46.5 us (8%)
  other arithmetic  16 us (3%)
  between operations  15 us (3%)
    reduce_scatter x2, waiting for transfers between devices, per_device(): lax.psum_scatter(jnp.dot(attended, out_weight, preferred_element_type=jnp...  166 us
    all_gather x2, waiting for transfers between devices, per_device(): lax.all_gather(normed, 'dp', axis=0, tiled=True)  124 us
    all_gather x2, waiting for transfers between devices, per_device(): key_piece = lax.all_gather(key_rows, 'frame', axis=0, tiled=True)  68.8 us
    all_gather x2, waiting for transfers between devices, per_device(): value_piece = lax.all_gather(value_rows, 'frame', axis=0, tiled=True)  37.9 us
    dot_general x2, matrix products, per_device(): jnp.einsum('qhd,khd->hqk', queries, key_piece.reshape(key_count, heads_de...  30.2 us
    dot_general x2, matrix products, per_device(): jnp.einsum('hqk,khd->qhd', weights.astype(jnp.bfloat16), value_piece.resh...  25.7 us
    dot_general x2, matrix products, per_device(): jnp.dot(lax.all_gather(normed, 'dp', axis=0, tiled=True), weights_flat, p...  20 us
    unnamed x10, local copies, waits for them, and re-layouts  16.9 us
  transfers between devices with their start and end apart: 8, of which 8 were waited for; matrix products, arithmetic and copies ran while one was open for 11% of the time, Pallas kernels for 0%

commit v1 on v0

v1 whole, which is shorter than its diff:
```python
import math

import jax
import jax.numpy as jnp
from jax import lax
from jax.experimental import pallas as pl
from jax.experimental.pallas import tpu as pltpu
from jax.sharding import PartitionSpec as P

HEAD = 128
STEPS = 2
EPSILON = 1e-06
ROWS = 16
VMEM = 56 * 1024 * 1024
GROUP = 8
FRAMES = 16


def over_dp(value, to):
    return lax.ppermute(value, "dp", [(d, to(d) % GROUP) for d in range(GROUP)])


def over_frame(value, to):
    return lax.ppermute(value, "frame", [(f, to(f) % FRAMES) for f in range(FRAMES)])


def gathered(block):
    beside = over_dp(block, lambda d: d ^ 1)
    below = over_dp(block, lambda d: d + 2)
    above = over_dp(block, lambda d: d - 2)
    across = over_dp(block, lambda d: d + 4)
    beside_below = over_dp(beside, lambda d: d + 2)
    beside_above = over_dp(beside, lambda d: d - 2)
    beside_across = over_dp(across, lambda d: d ^ 1)
    return [block, beside, below, above, across, beside_below, beside_above, beside_across]


def origins(d):
    other = d ^ 1
    return [
        d,
        other,
        (d + 6) % GROUP,
        (d + 2) % GROUP,
        (d + 4) % GROUP,
        (other + 6) % GROUP,
        (other + 2) % GROUP,
        (other + 4) % GROUP,
    ]


def normed_rows(x, scale, shift):
    centered = x - jnp.mean(x, axis=-1, keepdims=True)
    variance = jnp.mean(centered * centered, axis=-1, keepdims=True)
    return (centered * lax.rsqrt(variance + EPSILON) * (1.0 + scale) + shift).astype(jnp.bfloat16)


def project(normed, w_ref, q_ref, kv_ref):
    turn = pl.program_id(0)
    product = jnp.dot(normed[...], w_ref[0], preferred_element_type=jnp.float32)

    def head_normed(block):
        return block * lax.rsqrt(jnp.mean(block * block, axis=-1, keepdims=True) + EPSILON)

    heads = [slice(low, low + HEAD) for low in range(0, product.shape[1], HEAD)]

    @pl.when(turn == 0)
    def _():
        for cut in heads:
            kv_ref[0, :, cut] = head_normed(product[:, cut]).astype(jnp.bfloat16)

    @pl.when(turn == 1)
    def _():
        kv_ref[0] = product.astype(jnp.bfloat16)

    @pl.when(turn == 2)
    def _():
        for cut in heads:
            q_ref[:, cut] = head_normed(product[:, cut]).astype(jnp.bfloat16)


def qkv_from_rows(info, *refs):
    blocks, (mod_ref, w_ref, q_ref, kv_ref, own_ref, normed) = refs[:GROUP], refs[GROUP:]
    own_rows = blocks[0].shape[0]
    width = own_ref.shape[1]

    @pl.when(pl.program_id(0) == 0)
    def _():
        columns = pl.ds(pl.multiple_of(info[1] * width, HEAD), width)
        for index, block in enumerate(blocks):
            first = info[1 + index] * own_rows
            own_ref[pl.ds(pl.multiple_of(first, ROWS), own_rows), :] = block[:, columns]

            def one(step, carry, block=block, first=first):
                low = pl.multiple_of(step * ROWS, ROWS)
                x = block[pl.ds(low, ROWS), :].astype(jnp.float32)
                normed[pl.ds(pl.multiple_of(first + low, ROWS), ROWS), :] = normed_rows(
                    x, mod_ref[0, 1:2, :], mod_ref[0, 0:1, :]
                )
                return carry

            lax.fori_loop(0, own_rows // ROWS, one, 0)

    project(normed, w_ref, q_ref, kv_ref)


def qkv_from_columns(info, *refs):
    blocks, (mod_ref, w_ref, q_ref, kv_ref, normed) = refs[:GROUP], refs[GROUP:]
    rows, width = blocks[0].shape
    total = width * GROUP

    @pl.when(pl.program_id(0) == 0)
    def _():
        places = [
            pl.ds(pl.multiple_of(info[1 + index] * width, HEAD), width) for index in range(GROUP)
        ]

        def one(step, carry):
            band = pl.ds(pl.multiple_of(step * ROWS, ROWS), ROWS)
            parts = [block[band, :].astype(jnp.float32) for block in blocks]
            mean = sum(jnp.sum(part, axis=-1, keepdims=True) for part in parts) / total
            parts = [part - mean for part in parts]
            variance = (
                sum(jnp.sum(part * part, axis=-1, keepdims=True) for part in parts) / total
            )
            factor = lax.rsqrt(variance + EPSILON)
            for part, place in zip(parts, places):
                normed[band, place] = (
                    part * factor * (1.0 + mod_ref[0, 1:2, place]) + mod_ref[0, 0:1, place]
                ).astype(jnp.bfloat16)
            return carry

        lax.fori_loop(0, rows // ROWS, one, 0)

    project(normed, w_ref, q_ref, kv_ref)


def qkv(blocks, by_rows, info, mod_table, weights):
    width, inner = weights.shape[1:]
    rows = blocks[0].shape[0] * (GROUP if by_rows else 1)
    whole = lambda shape: pl.BlockSpec(shape, lambda j, info: (0,) * len(shape))
    out_shape = [
        jax.ShapeDtypeStruct((rows, inner), jnp.bfloat16),
        jax.ShapeDtypeStruct((2, rows, inner), jnp.bfloat16),
    ]
    out_specs = [
        whole((rows, inner)),
        pl.BlockSpec((1, rows, inner), lambda j, info: (jnp.minimum(j, 1), 0, 0)),
    ]
    if by_rows:
        out_shape.append(jax.ShapeDtypeStruct((rows, width // GROUP), jnp.bfloat16))
        out_specs.append(whole((rows, width // GROUP)))
    return pl.pallas_call(
        qkv_from_rows if by_rows else qkv_from_columns,
        out_shape=out_shape,
        grid_spec=pltpu.PrefetchScalarGridSpec(
            num_scalar_prefetch=1,
            grid=(3,),
            in_specs=[whole(block.shape) for block in blocks]
            + [
                pl.BlockSpec((1, 3, width), lambda j, info: (info[0], 0, 0)),
                pl.BlockSpec((1, width, inner), lambda j, info: ((j + 1) % 3, 0, 0)),
            ],
            out_specs=out_specs,
            scratch_shapes=[pltpu.VMEM((rows, width), jnp.bfloat16)],
        ),
        compiler_params=pltpu.CompilerParams(vmem_limit_bytes=VMEM),
        cost_estimate=pl.CostEstimate(
            flops=6 * rows * width * inner,
            bytes_accessed=6 * width * inner + 2 * rows * width,
            transcendentals=0,
        ),
        name="qkv",
    )(info, *blocks, mod_table, weights)


def attend_kernel(info, qa_ref, qb_ref, *refs):
    kv = [(refs[2 * i], refs[2 * i + 1]) for i in range(4)]
    keep_ref, keep_sum_ref, send_ref, acc = refs[8:]
    head, half = pl.program_id(0), pl.program_id(1)
    rows = qa_ref.shape[0]
    inner = keep_ref.shape[1]
    factor = math.log2(math.e) / math.sqrt(HEAD)
    band = pl.ds(pl.multiple_of(half * rows, ROWS), rows)
    place = pl.ds(pl.multiple_of(head * HEAD, HEAD), HEAD)
    lanes = lax.broadcasted_iota(jnp.int32, (rows, HEAD), 1)
    for side, q_ref in enumerate((qa_ref, qb_ref)):
        acc[...] = jnp.zeros_like(acc)
        rank = info[side * 2 + half]
        for index, (k_ref, v_ref) in enumerate(kv):

            @pl.when(info[4 + index] <= rank)
            def _(q_ref=q_ref, k_ref=k_ref, v_ref=v_ref):
                scores = lax.dot_general(
                    q_ref[...],
                    k_ref[0],
                    (((1,), (1,)), ((), ())),
                    preferred_element_type=jnp.float32,
                )
                weights = jnp.exp2(scores * factor).astype(jnp.bfloat16)
                values = v_ref[0]
                acc[...] += jnp.dot(
                    weights,
                    jnp.concatenate([values, jnp.ones_like(values)], axis=1),
                    preferred_element_type=jnp.float32,
                )

        total = acc[:, HEAD:]
        if side == 0:
            keep_ref[band, place] = acc[:, :HEAD]

            @pl.when(head == 0)
            def _():
                keep_sum_ref[band, :] = jnp.where(lanes == 0, total, 0.0)

            @pl.when(head > 0)
            def _():
                keep_sum_ref[band, :] = jnp.where(lanes == head, total, keep_sum_ref[band, :])
        else:
            send_ref[band, place] = acc[:, :HEAD].astype(jnp.bfloat16)
            coarse = total.astype(jnp.bfloat16)
            fine = (total - coarse.astype(jnp.float32)).astype(jnp.bfloat16)
            pair = jnp.where(
                lanes == head,
                coarse.astype(jnp.float32),
                jnp.where(lanes == head + 3, fine.astype(jnp.float32), 0.0),
            )

            @pl.when(head == 0)
            def _():
                send_ref[band, inner:] = pair.astype(jnp.bfloat16)

            @pl.when(head > 0)
            def _():
                send_ref[band, inner:] = (
                    pair + send_ref[band, inner:].astype(jnp.float32)
                ).astype(jnp.bfloat16)


def attend(qa, qb, kvs, info):
    rows = qa.shape[0] // 2
    inner = qa.shape[1]
    whole = lambda shape: pl.BlockSpec(shape, lambda h, i, info: (0,) * len(shape))
    specs, operands = [], []
    for kv in kvs:
        for which in range(2):
            specs.append(
                pl.BlockSpec((1, rows, HEAD), lambda h, i, info, which=which: (which, 0, h))
            )
            operands.append(kv)
    return pl.pallas_call(
        attend_kernel,
        out_shape=[
            jax.ShapeDtypeStruct((2 * rows, inner), jnp.float32),
            jax.ShapeDtypeStruct((2 * rows, HEAD), jnp.float32),
            jax.ShapeDtypeStruct((2 * rows, inner + HEAD), jnp.bfloat16),
        ],
        grid_spec=pltpu.PrefetchScalarGridSpec(
            num_scalar_prefetch=1,
            grid=(inner // HEAD, 2),
            in_specs=[pl.BlockSpec((rows, HEAD), lambda h, i, info: (i, h))] * 2 + specs,
            out_specs=[
                whole((2 * rows, inner)),
                whole((2 * rows, HEAD)),
                whole((2 * rows, inner + HEAD)),
            ],
            scratch_shapes=[pltpu.VMEM((rows, 2 * HEAD), jnp.float32)],
        ),
        compiler_params=pltpu.CompilerParams(vmem_limit_bytes=VMEM),
        cost_estimate=pl.CostEstimate(
            flops=64 * rows * rows * inner,
            bytes_accessed=32 * rows * inner,
            transcendentals=16 * rows * rows * 3,
        ),
        name="attend",
    )(info, qa, qb, *operands)


def received_sums(ref, inner):
    pair = ref[:, inner:].astype(jnp.float32)
    return pair + pltpu.roll(pair, HEAD - 3, 1)


def over_cores_kernel(keep_ref, keep_sum_ref, got_ref, own_ref, own_sum_ref, send_ref):
    rows, inner = own_ref.shape
    own, other = slice(0, rows), slice(rows, 2 * rows)
    sums = keep_sum_ref[...] + received_sums(got_ref, inner)
    own_ref[...] = keep_ref[own, :] + got_ref[own, :inner].astype(jnp.float32)
    own_sum_ref[...] = sums[own, :]
    send_ref[:, :inner] = (
        keep_ref[other, :] + got_ref[other, :inner].astype(jnp.float32)
    ).astype(jnp.bfloat16)
    lanes = lax.broadcasted_iota(jnp.int32, (rows, HEAD), 1)
    theirs = sums[other, :]
    coarse = theirs.astype(jnp.bfloat16).astype(jnp.float32)
    send_ref[:, inner:] = jnp.where(
        lanes < 3, coarse, pltpu.roll(theirs - coarse, 3, 1)
    ).astype(jnp.bfloat16)


def over_cores(keep, keep_sum, got):
    rows, inner = keep.shape[0] // 2, keep.shape[1]
    return pl.pallas_call(
        over_cores_kernel,
        out_shape=[
            jax.ShapeDtypeStruct((rows, inner), jnp.float32),
            jax.ShapeDtypeStruct((rows, HEAD), jnp.float32),
            jax.ShapeDtypeStruct((rows, inner + HEAD), jnp.bfloat16),
        ],
        compiler_params=pltpu.CompilerParams(vmem_limit_bytes=VMEM),
        name="over_cores",
    )(keep, keep_sum, got)


def finish_kernel(own_ref, own_sum_ref, got_ref, out_ref):
    inner = own_ref.shape[1]
    sums = own_sum_ref[...] + received_sums(got_ref, inner)
    for head in range(inner // HEAD):
        cut = slice(head * HEAD, (head + 1) * HEAD)
        out_ref[:, cut] = (
            (own_ref[:, cut] + got_ref[:, cut].astype(jnp.float32)) / sums[:, head : head + 1]
        ).astype(jnp.bfloat16)


def finish(own, own_sum, got):
    return pl.pallas_call(
        finish_kernel,
        out_shape=jax.ShapeDtypeStruct(own.shape, jnp.bfloat16),
        compiler_params=pltpu.CompilerParams(vmem_limit_bytes=VMEM),
        name="finish",
    )(own, own_sum, got)


def branch_kernel(info, *refs):
    parts, (w_ref, hidden_ref, mod_ref, out_ref) = refs[:GROUP], refs[GROUP:]
    width = hidden_ref.shape[1]
    total = None
    for index, part in enumerate(parts):
        term = jnp.dot(part[...], w_ref[info[1 + index]], preferred_element_type=jnp.float32)
        total = term if total is None else total + term
    columns = pl.ds(pl.multiple_of(info[1] * width, HEAD), width)
    out_ref[...] = (hidden_ref[...].astype(jnp.float32) + mod_ref[0, 2:3, columns] * total).astype(
        jnp.bfloat16
    )


def add_branch(parts, weights, hidden, mod_table, info):
    whole = lambda shape: pl.BlockSpec(shape, lambda j, info: (0,) * len(shape))
    full = mod_table.shape[2]
    return pl.pallas_call(
        branch_kernel,
        out_shape=jax.ShapeDtypeStruct(hidden.shape, jnp.bfloat16),
        grid_spec=pltpu.PrefetchScalarGridSpec(
            num_scalar_prefetch=1,
            grid=(1,),
            in_specs=[whole(part.shape) for part in parts]
            + [
                whole(weights.shape),
                whole(hidden.shape),
                pl.BlockSpec((1, 3, full), lambda j, info: (info[0], 0, 0)),
            ],
            out_specs=whole(hidden.shape),
        ),
        compiler_params=pltpu.CompilerParams(vmem_limit_bytes=VMEM),
        name="add_branch",
    )(info, *parts, weights, hidden, mod_table)


def out_columns(out_weight, core, after):
    rows, width = out_weight.shape
    half = rows // 2
    own = lax.dynamic_slice(out_weight, (core * half, 0), (half, width))
    own = jnp.transpose(own.reshape(half, GROUP, width // GROUP), (1, 0, 2))
    own, after = lax.optimization_barrier((own, after))
    mine = lax.all_to_all(own, "dp", 0, 0, tiled=True)
    theirs = over_frame(mine, lambda f: f ^ 1)
    first = core == 0
    return jnp.concatenate(
        [jnp.where(first, mine, theirs), jnp.where(first, theirs, mine)], axis=1
    )


def per_device(tokens, qkv_weight, out_weight, mod_table, levels, frame_order):
    own_rows, width = tokens.shape
    frame = lax.axis_index("frame")
    place = lax.axis_index("dp")
    level = levels[frame]
    where = origins(place)
    rank = lambda f: frame_order[f % FRAMES]
    ranks = jnp.stack(
        [
            rank(frame),
            rank(frame ^ 2),
            rank(frame ^ 1),
            rank(frame ^ 3),
            rank(frame),
            rank(frame + 12),
            rank(frame + 4),
            rank(frame + 8),
        ]
    ).astype(jnp.int32)
    blocks = gathered(tokens)
    weights = jnp.transpose(qkv_weight, (1, 0, 2))
    own_hidden = None
    out_weights = None
    attended = None
    for step_index in range(STEPS):
        info = jnp.stack([level + step_index] + where).astype(jnp.int32)
        if step_index == 0:
            q, kv, own_hidden = qkv(blocks, True, info, mod_table, weights)
        else:
            q, kv = qkv(blocks, False, info, mod_table, weights)
        kvs = [
            kv,
            over_frame(kv, lambda f: f + 4),
            over_frame(kv, lambda f: f - 4),
            over_frame(kv, lambda f: f + 8),
        ]
        qa = jnp.concatenate([q, over_frame(q, lambda f: f ^ 2)], axis=0)
        qb = over_frame(qa, lambda f: f ^ 1)
        if step_index == 0:
            out_weights = out_columns(out_weight, frame % 2, kv)
        keep, keep_sum, send = attend(qa, qb, kvs, ranks)
        own, own_sum, send = over_cores(keep, keep_sum, over_frame(send, lambda f: f ^ 1))
        attended = finish(own, own_sum, over_frame(send, lambda f: f ^ 2))
        own_hidden = add_branch(gathered(attended), out_weights, own_hidden, mod_table, info)
        if step_index < STEPS - 1:
            blocks = gathered(own_hidden)
    pieces = own_hidden.reshape(GROUP, own_rows, width // GROUP)
    pieces = lax.all_to_all(pieces, "dp", 0, 0, tiled=True)
    hidden = jnp.transpose(pieces, (1, 0, 2)).reshape(own_rows, width)
    return (hidden, attended)


def solution(mesh):
    return jax.shard_map(
        per_device,
        mesh=mesh,
        in_specs=(P(("frame", "dp"), None), P(None, None, "dp"), P("dp", None), P(), P(), P()),
        out_specs=(P(("frame", "dp"), None), P("frame", "dp")),
        check_vma=False,
    )
```

time: 561 us -> 364 us (0.65)
  waiting for transfers between devices: 397 us -> 134 us
  Pallas kernels: 0 us -> 93.2 us
  starting transfers between devices: 0.51 us -> 90.2 us
  matrix products: 84.1 us -> 0 us
  local copies, waits for them, and re-layouts: 46.5 us -> 26.8 us
  blocking collectives: 0 us -> 15.1 us
  between operations: 15 us -> 1.68 us
  other arithmetic: 16 us -> 4.16 us
    all_gather x6 -> x0, waiting for transfers between devices: 231 us -> none  [the longest x2 124 us: per_device(): lax.all_gather(normed, 'dp', axis=0, tiled=True)]
    reduce_scatter x2 -> x0, waiting for transfers between devices: 166 us -> none  [per_device(): lax.psum_scatter(jnp.dot(attended, out_weight, preferred_element_type=jnp...]
    ppermute x0 -> x43, waiting for transfers between devices: none -> 134 us  [the longest x15 70.8 us: over_frame(): lax.ppermute(value, 'frame', [(f, to(f) % FRAMES) for f in range(FRAMES)])]
    pallas_call x0 -> x10, Pallas kernels: none -> 93.2 us  [the longest x2 38.3 us: qkv(): pl.pallas_call(qkv_from_rows if by_rows else qkv_from_columns, out_shape=...]
    ppermute x0 -> x43, starting transfers between devices: none -> 86.1 us  [the longest x28 52.5 us: over_dp(): return lax.ppermute(value, 'dp', [(d, to(d) % GROUP) for d in range(GROUP)])]
    dot_general x8 -> x0, matrix products: 84.1 us -> none  [the longest x2 30.2 us: per_device(): jnp.einsum('qhd,khd->hqk', queries, key_piece.reshape(key_count, heads_de...]
    all_gather x4 -> x0, local copies, waits for them, and re-layouts: 26.6 us -> none  [the longest x2 13.3 us: per_device(): key_piece = lax.all_gather(key_rows, 'frame', axis=0, tiled=True)]
    all_to_all x0 -> x1, blocking collectives: none -> 15.1 us  [per_device(): pieces = lax.all_to_all(pieces, 'dp', 0, 0, tiled=True)]
  transfers between devices with their start and end apart: 8 -> 44, of which waited for: 8 -> 25; matrix products, arithmetic and copies ran while one was open for 11% -> 5% of each run, Pallas kernels for 0% -> 6%
where the time goes in v1:
time: 364 us; the launch traced here: 365 us
  waiting for transfers between devices  134 us (37%)
  Pallas kernels  93.2 us (26%)
  starting transfers between devices  90.2 us (25%)
  local copies, waits for them, and re-layouts  26.8 us (7%)
  blocking collectives  15.1 us (4%)
  other arithmetic  4.16 us (1%)
    ppermute x15, waiting for transfers between devices, over_frame(): lax.ppermute(value, 'frame', [(f, to(f) % FRAMES) for f in range(FRAMES)])  70.8 us
    ppermute x28, waiting for transfers between devices, over_dp(): return lax.ppermute(value, 'dp', [(d, to(d) % GROUP) for d in range(GROUP)])  62.9 us
    ppermute x28, starting transfers between devices, over_dp(): return lax.ppermute(value, 'dp', [(d, to(d) % GROUP) for d in range(GROUP)])  52.5 us
    pallas_call x2, Pallas kernels, qkv(): pl.pallas_call(qkv_from_rows if by_rows else qkv_from_columns, out_shape=...  38.3 us
    ppermute x15, starting transfers between devices, over_frame(): lax.ppermute(value, 'frame', [(f, to(f) % FRAMES) for f in range(FRAMES)])  33.6 us
    pallas_call x2, Pallas kernels, attend(): pl.pallas_call(attend_kernel, out_shape=[jax.ShapeDtypeStruct((2 * rows,...  30.8 us
    all_to_all x1, blocking collectives, per_device(): pieces = lax.all_to_all(pieces, 'dp', 0, 0, tiled=True)  15.1 us
    unnamed x87, local copies, waits for them, and re-layouts  13.8 us
  transfers between devices with their start and end apart: 44, of which 25 were waited for; matrix products, arithmetic and copies ran while one was open for 5% of the time, Pallas kernels for 6%

profile of v1, /device:TPU:0, one launch (start us, length us, event | category | flops | bytes accessed | tf_op | source)
XLA Modules:
  0.0 364.8 jit_solution(3354189490710772581)
XLA Ops:
  0.6 3.4 collective-permute-start
  4.0 3.9 %collective-permute-start.3 = (bf16[48,5120]{1,0:T(8,128)(2,1)}, bf16[48,5120]{1,0:T(8,128)(2,1)S(1)}, u32[]{:S(2)}, u32[]{:S(2)}) collective-permute-start(bf16[48,5120]{1,0:T(8,128)(2,1)} %refs_0_.1), channel_id=1, source_target_pairs={{0,4},{1,5},{2,6},{3,7},{4,0},{5,1},{6,2},{7,3},{8,12},{9,13},{10,... | collective-permute-start | bytes 1474568 | tf_op jit(solution)/shard_map/ppermute | solution.py:20
  31.8 8.3 %collective-permute-done.4.refs_5_ = bf16[48,5120]{1,0:T(8,128)(2,1)S(1)} collective-permute-done((bf16[48,5120]{1,0:T(8,128)(2,1)S(1)}, bf16[48,5120]{1,0:T(8,128)(2,1)S(1)}, u32[]{:S(2)}, u32[]{:S(2)}) %collective-permute-start.4) | collective-permute-done | bytes 491552 | tf_op jit(solution)/shard_map/ppermute | solution.py:20
  41.9 19.5 %qkv.2 = (bf16[384,384]{1,0:T(8,128)(2,1)}, bf16[2,384,384]{2,1,0:T(8,128)(2,1)}, bf16[384,640]{1,0:T(8,128)(2,1)}) custom-call(s32[9]{0:T(128)} %stack.52.info, bf16[48,5120]{1,0:T(8,128)(2,1)} %refs_0_.1, bf16[48,5120]{1,0:T(8,128)(2,1)} %copy-done.27, bf16[48,5120]{1,0:T(8,128)(2,1)} %copy-done.29, bf16[48,5120]{1,0:T(8,128)(2,1)} %copy-done.30, ...), custom_call_target="tpu_custom_call" | custom-call | flops 4529848320 | bytes 15728640 | tf_op jit(solution)/shard_map/qkv/pallas_call | solution.py:153
  61.4 4.0 %all-to-all-start = ((bf16[8,192,640]{2,1,0:T(8,128)(2,1)}), bf16[8,192,640]{2,1,0:T(8,128)(2,1)S(1)}, u32[]{:S(2)}, u32[]{:S(2)}) async-start(bf16[8,192,640]{2,1,0:T(8,128)(2,1)} %bitcast.19), calls=%async_computation | async-start | bytes 3932160 | tf_op jit(solution)/shard_map/all_to_all | solution.py:375
  71.4 23.7 %collective-permute-done.7 = bf16[384,384]{1,0:T(8,128)(2,1)S(1)} collective-permute-done((bf16[384,384]{1,0:T(8,128)(2,1)S(1)}, bf16[384,384]{1,0:T(8,128)(2,1)S(1)}, u32[]{:S(2)}, u32[]{:S(2)}) %collective-permute-start.7) | collective-permute-done | bytes 294944 | tf_op jit(solution)/shard_map/ppermute | solution.py:24
  96.4 5.6 %stack.51.info = s32[8]{0:T(128)} concatenate(s32[1]{0:T(128)} %get-tuple-element.45, s32[1]{0:T(128)} %get-tuple-element.44, s32[1]{0:T(128)} %get-tuple-element.43, s32[1]{0:T(128)} %get-tuple-element.42, s32[1]{0:T(128)} %get-tuple-element.45, s32[1]{0:T(128)} %get-tuple-element.41, s32[1]{0:T(128)} %get-tuple-element.46, s32[1]{0:T(128)} %get-tuple-element.40), dimensions={0} | concatenate | bytes 64 | tf_op jit(solution)/shard_map/stack | solution.py:390
  102.1 15.4 %attend.2 = (f32[768,384]{1,0:T(8,128)}, f32[768,128]{1,0:T(8,128)}, bf16[768,512]{1,0:T(8,128)(2,1)}) custom-call(s32[8]{0:T(128)} %stack.51.info, bf16[768,384]{1,0:T(8,128)(2,1)} %copy-done.19, bf16[768,384]{1,0:T(8,128)(2,1)} %collective-permute-done.8.qb_ref, bf16[2,384,384]{2,1,0:T(8,128)(2,1)} %get-tuple-element.21.refs_0_.refs_1_, ...), custom_call_target="tpu_custom_call" | custom-call | flops 3623878656 | bytes 4718592 | tf_op jit(solution)/shard_map/attend/pallas_call | solution.py:251
  117.5 3.2 collective-permute-start.12
  126.5 8.1 %collective-permute-start.13 = (bf16[384,512]{1,0:T(8,128)(2,1)}, bf16[384,512]{1,0:T(8,128)(2,1)S(1)}, u32[]{:S(2)}, u32[]{:S(2)}) collective-permute-start(bf16[384,512]{1,0:T(8,128)(2,1)} %get-tuple-element.27), channel_id=1, source_target_pairs={{0,16},{8,24},{16,0},{24,8},{32,48},{40,56},{48,32},{56,40},{64,80... | collective-permute-start | bytes 1179656 | tf_op jit(solution)/shard_map/ppermute | solution.py:24
  134.7 9.8 %collective-permute-done.13.got_ref = bf16[384,512]{1,0:T(8,128)(2,1)S(1)} collective-permute-done((bf16[384,512]{1,0:T(8,128)(2,1)}, bf16[384,512]{1,0:T(8,128)(2,1)S(1)}, u32[]{:S(2)}, u32[]{:S(2)}) %collective-permute-start.13) | collective-permute-done | bytes 393248 | tf_op jit(solution)/shard_map/ppermute | solution.py:24
  147.6 3.7 %collective-permute-start.14 = (bf16[384,384]{1,0:T(8,128)(2,1)}, bf16[384,384]{1,0:T(8,128)(2,1)S(1)}, u32[]{:S(2)}, u32[]{:S(2)}) collective-permute-start(bf16[384,384]{1,0:T(8,128)(2,1)} %finish.2.refs_0_), channel_id=1, source_target_pairs={{0,1},{1,0},{2,3},{3,2},{4,5},{5,4},{6,7},{7,6},{8,9},{9,8},{10,11... | collective-permute-start | bytes 884744 | tf_op jit(solution)/shard_map/ppermute | solution.py:20
  154.1 3.2 collective-permute-start.16
  159.5 3.4 collective-permute-done.17.refs_4_
  169.8 4.2 %collective-permute-done.18.refs_5_ = bf16[384,384]{1,0:T(8,128)(2,1)S(1)} collective-permute-done((bf16[384,384]{1,0:T(8,128)(2,1)S(1)}, bf16[384,384]{1,0:T(8,128)(2,1)S(1)}, u32[]{:S(2)}, u32[]{:S(2)}) %collective-permute-start.18) | collective-permute-done | bytes 294944 | tf_op jit(solution)/shard_map/ppermute | solution.py:20
  174.9 6.9 %add_branch.2.refs_0_.refs_9_ = bf16[384,640]{1,0:T(8,128)(2,1)} custom-call(s32[9]{0:T(128)} %stack.52.info, bf16[384,384]{1,0:T(8,128)(2,1)} %finish.2.refs_0_, bf16[384,384]{1,0:T(8,128)(2,1)} %copy-done.4, bf16[384,384]{1,0:T(8,128)(2,1)} %copy-done.6, bf16[384,384]{1,0:T(8,128)(2,1)} %copy-done.7, bf16[384,384]{1,0:T(8,128)(2,1)} %copy-done.5, ...), custom_call_target="tpu_custom_call" | custom-call | tf_op jit(solution)/shard_map/add_branch/pallas_call | solution.py:350
  187.2 9.5 %collective-permute-done.22.refs_1_ = bf16[384,640]{1,0:T(8,128)(2,1)S(1)} collective-permute-done((bf16[384,640]{1,0:T(8,128)(2,1)}, bf16[384,640]{1,0:T(8,128)(2,1)S(1)}, u32[]{:S(2)}, u32[]{:S(2)}) %collective-permute-start.22) | collective-permute-done | bytes 491552 | tf_op jit(solution)/shard_map/ppermute | solution.py:20
  202.6 4.7 %collective-permute-done.23.refs_2_ = bf16[384,640]{1,0:T(8,128)(2,1)S(1)} collective-permute-done((bf16[384,640]{1,0:T(8,128)(2,1)}, bf16[384,640]{1,0:T(8,128)(2,1)S(1)}, u32[]{:S(2)}, u32[]{:S(2)}) %collective-permute-start.23) | collective-permute-done | bytes 491552 | tf_op jit(solution)/shard_map/ppermute | solution.py:20
  208.2 9.6 %collective-permute-done.26.refs_5_ = bf16[384,640]{1,0:T(8,128)(2,1)S(1)} collective-permute-done((bf16[384,640]{1,0:T(8,128)(2,1)S(1)}, bf16[384,640]{1,0:T(8,128)(2,1)S(1)}, u32[]{:S(2)}, u32[]{:S(2)}) %collective-permute-start.26) | collective-permute-done | bytes 491552 | tf_op jit(solution)/shard_map/ppermute | solution.py:20
  219.6 18.8 %qkv.3 = (bf16[384,384]{1,0:T(8,128)(2,1)}, bf16[2,384,384]{2,1,0:T(8,128)(2,1)}) custom-call(s32[9]{0:T(128)} %stack.50.info, bf16[384,640]{1,0:T(8,128)(2,1)} %add_branch.2.refs_0_.refs_9_, bf16[384,640]{1,0:T(8,128)(2,1)} %copy-done.34, bf16[384,640]{1,0:T(8,128)(2,1)} %copy-done.36, bf16[384,640]{1,0:T(8,128)(2,1)} %copy-done.37, ...), custom_call_target="tpu_custom_call" | custom-call | flops 4529848320 | bytes 15728640 | tf_op jit(solution)/shard_map/qkv/pallas_call | solution.py:153
  239.4 3.2 collective-permute-start.32
  247.6 20.8 %collective-permute-done.31.refs_2_.refs_3_ = bf16[2,384,384]{2,1,0:T(8,128)(2,1)S(1)} collective-permute-done((bf16[2,384,384]{2,1,0:T(8,128)(2,1)}, bf16[2,384,384]{2,1,0:T(8,128)(2,1)S(1)}, u32[]{:S(2)}, u32[]{:S(2)}) %collective-permute-start.31) | collective-permute-done | bytes 589856 | tf_op jit(solution)/shard_map/ppermute | solution.py:24
  270.5 15.4 %attend.3 = (f32[768,384]{1,0:T(8,128)}, f32[768,128]{1,0:T(8,128)}, bf16[768,512]{1,0:T(8,128)(2,1)}) custom-call(s32[8]{0:T(128)} %stack.51.info, bf16[768,384]{1,0:T(8,128)(2,1)} %copy-done.20, bf16[768,384]{1,0:T(8,128)(2,1)} %copy-done.26, bf16[2,384,384]{2,1,0:T(8,128)(2,1)} %get-tuple-element.31.refs_0_.refs_1_, ...), custom_call_target="tpu_custom_call" | custom-call | flops 3623878656 | bytes 4718592 | tf_op jit(solution)/shard_map/attend/pallas_call | solution.py:251
  290.4 2.9 over_cores.3
  293.3 8.7 %collective-permute-start.35 = (bf16[384,512]{1,0:T(8,128)(2,1)}, bf16[384,512]{1,0:T(8,128)(2,1)S(1)}, u32[]{:S(2)}, u32[]{:S(2)}) collective-permute-start(bf16[384,512]{1,0:T(8,128)(2,1)} %get-tuple-element.37), channel_id=1, source_target_pairs={{0,16},{8,24},{16,0},{24,8},{32,48},{40,56},{48,32},{56,40},{64,80... | collective-permute-start | bytes 1179656 | tf_op jit(solution)/shard_map/ppermute | solution.py:24
  301.9 9.6 %collective-permute-done.35.got_ref = bf16[384,512]{1,0:T(8,128)(2,1)S(1)} collective-permute-done((bf16[384,512]{1,0:T(8,128)(2,1)}, bf16[384,512]{1,0:T(8,128)(2,1)S(1)}, u32[]{:S(2)}, u32[]{:S(2)}) %collective-permute-start.35) | collective-permute-done | bytes 393248 | tf_op jit(solution)/shard_map/ppermute | solution.py:24
  314.6 3.2 collective-permute-start.36
  321.7 3.2 collective-permute-done.36.refs_1_
  331.3 2.9 collective-permute-done.37.refs_2_
  334.7 5.7 %collective-permute-done.40.refs_5_ = bf16[384,384]{1,0:T(8,128)(2,1)S(1)} collective-permute-done((bf16[384,384]{1,0:T(8,128)(2,1)S(1)}, bf16[384,384]{1,0:T(8,128)(2,1)S(1)}, u32[]{:S(2)}, u32[]{:S(2)}) %collective-permute-start.40) | collective-permute-done | bytes 294944 | tf_op jit(solution)/shard_map/ppermute | solution.py:20
  342.0 6.9 %add_branch.3 = bf16[384,640]{1,0:T(8,128)(2,1)} custom-call(s32[9]{0:T(128)} %stack.50.info, bf16[384,384]{1,0:T(8,128)(2,1)} %finish.3.refs_0_, bf16[384,384]{1,0:T(8,128)(2,1)} %copy-done.8, bf16[384,384]{1,0:T(8,128)(2,1)} %copy-done.11, bf16[384,384]{1,0:T(8,128)(2,1)} %copy-done.13, bf16[384,384]{1,0:T(8,128)(2,1)} %copy-done.10, ...), custom_call_target="tpu_custom_call" | custom-call | tf_op jit(solution)/shard_map/add_branch/pallas_call | solution.py:350
  348.9 15.1 %all_to_all.10 = bf16[8,48,640]{2,1,0:T(8,128)(2,1)S(1)} all-to-all(bf16[8,48,640]{2,1,0:T(8,128)(2,1)} %bitcast.21), channel_id=1, replica_groups=mesh['frame'=16,'dp'=8] {'dp'}, dimensions={0} | all-to-all | bytes 983040 | tf_op jit(solution)/shard_map/all_to_all | solution.py:430
  (166 shorter events, 96.5 us)
Async XLA Ops:
  0.6 14.8 %collective-permute-start = (bf16[48,5120]{1,0:T(8,128)(2,1)}, bf16[48,5120]{1,0:T(8,128)(2,1)S(1)}, u32[]{:S(2)}, u32[]{:S(2)}) collective-permute-start(bf16[48,5120]{1,0:T(8,128)(2,1)} %refs_0_.1), channel_id=1, source_target_pairs={{0,1},{1,0},{2,3},{3,2},{4,5},{5,4},{6,7},{7,6},{8,9},{9,8},{10,11... | collective-permute-start | bytes 1474568 | tf_op jit(solution)/shard_map/ppermute | solution.py:20
  4.0 16.2 %collective-permute-start.3 = (bf16[48,5120]{1,0:T(8,128)(2,1)}, bf16[48,5120]{1,0:T(8,128)(2,1)S(1)}, u32[]{:S(2)}, u32[]{:S(2)}) collective-permute-start(bf16[48,5120]{1,0:T(8,128)(2,1)} %refs_0_.1), channel_id=1, source_target_pairs={{0,4},{1,5},{2,6},{3,7},{4,0},{5,1},{6,2},{7,3},{8,12},{9,13},{10,... | collective-permute-start | bytes 1474568 | tf_op jit(solution)/shard_map/ppermute | solution.py:20
  7.9 22.5 %collective-permute-start.1 = (bf16[48,5120]{1,0:T(8,128)(2,1)}, bf16[48,5120]{1,0:T(8,128)(2,1)S(1)}, u32[]{:S(2)}, u32[]{:S(2)}) collective-permute-start(bf16[48,5120]{1,0:T(8,128)(2,1)} %refs_0_.1), channel_id=1, source_target_pairs={{0,2},{1,3},{2,4},{3,5},{4,6},{5,7},{6,0},{7,1},{8,10},{9,11},{10,... | collective-permute-start | bytes 1474568 | tf_op jit(solution)/shard_map/ppermute | solution.py:20
  8.9 22.9 %collective-permute-start.2 = (bf16[48,5120]{1,0:T(8,128)(2,1)}, bf16[48,5120]{1,0:T(8,128)(2,1)S(1)}, u32[]{:S(2)}, u32[]{:S(2)}) collective-permute-start(bf16[48,5120]{1,0:T(8,128)(2,1)} %refs_0_.1), channel_id=1, source_target_pairs={{0,6},{1,7},{2,0},{3,1},{4,2},{5,3},{6,4},{7,5},{8,14},{9,15},{10,... | collective-permute-start | bytes 1474568 | tf_op jit(solution)/shard_map/ppermute | solution.py:20
  15.4 24.7 %collective-permute-start.4 = (bf16[48,5120]{1,0:T(8,128)(2,1)S(1)}, bf16[48,5120]{1,0:T(8,128)(2,1)S(1)}, u32[]{:S(2)}, u32[]{:S(2)}) collective-permute-start(bf16[48,5120]{1,0:T(8,128)(2,1)S(1)} %collective-permute-done.refs_1_), channel_id=1, source_target_pairs={{0,2},{1,3},{2,4},{3,5},{4,6},{5,7},{6,0},{7,1},{8,10},{9,11},{10,... | collective-permute-start | bytes 1474568 | tf_op jit(solution)/shard_map/ppermute | solution.py:20
  17.4 23.5 %collective-permute-start.5 = (bf16[48,5120]{1,0:T(8,128)(2,1)S(1)}, bf16[48,5120]{1,0:T(8,128)(2,1)S(1)}, u32[]{:S(2)}, u32[]{:S(2)}) collective-permute-start(bf16[48,5120]{1,0:T(8,128)(2,1)S(1)} %collective-permute-done.refs_1_), channel_id=1, source_target_pairs={{0,6},{1,7},{2,0},{3,1},{4,2},{5,3},{6,4},{7,5},{8,14},{9,15},{10,... | collective-permute-start | bytes 1474568 | tf_op jit(solution)/shard_map/ppermute | solution.py:20
  20.2 20.6 %collective-permute-start.6 = (bf16[48,5120]{1,0:T(8,128)(2,1)S(1)}, bf16[48,5120]{1,0:T(8,128)(2,1)S(1)}, u32[]{:S(2)}, u32[]{:S(2)}) collective-permute-start(bf16[48,5120]{1,0:T(8,128)(2,1)S(1)} %collective-permute-done.3.refs_4_), channel_id=1, source_target_pairs={{0,1},{1,0},{2,3},{3,2},{4,5},{5,4},{6,7},{7,6},{8,9},{9,8},{10,11... | collective-permute-start | bytes 1474568 | tf_op jit(solution)/shard_map/ppermute | solution.py:20
  61.4 33.9 %all-to-all-start = ((bf16[8,192,640]{2,1,0:T(8,128)(2,1)}), bf16[8,192,640]{2,1,0:T(8,128)(2,1)S(1)}, u32[]{:S(2)}, u32[]{:S(2)}) async-start(bf16[8,192,640]{2,1,0:T(8,128)(2,1)} %bitcast.19), calls=%async_computation | async-start | bytes 3932160 | tf_op jit(solution)/shard_map/all_to_all | solution.py:375
  65.5 29.7 %collective-permute-start.7 = (bf16[384,384]{1,0:T(8,128)(2,1)S(1)}, bf16[384,384]{1,0:T(8,128)(2,1)S(1)}, u32[]{:S(2)}, u32[]{:S(2)}) collective-permute-start(bf16[384,384]{1,0:T(8,128)(2,1)S(1)} %copy-done.18), channel_id=1, source_target_pairs={{0,16},{8,24},{16,0},{24,8},{32,48},{40,56},{48,32},{56,40},{64,80... | collective-permute-start | bytes 884744 | tf_op jit(solution)/shard_map/ppermute | solution.py:24
  66.9 35.1 %collective-permute-start.10 = (bf16[2,384,384]{2,1,0:T(8,128)(2,1)S(1)}, bf16[2,384,384]{2,1,0:T(8,128)(2,1)}, u32[]{:S(2)}, u32[]{:S(2)}) collective-permute-start(bf16[2,384,384]{2,1,0:T(8,128)(2,1)S(1)} %copy-done.22), channel_id=1, source_target_pairs={{0,96},{8,104},{16,112},{24,120},{32,0},{40,8},{48,16},{56,24},{64... | collective-permute-start | bytes 1769480 | tf_op jit(solution)/shard_map/ppermute | solution.py:24
  69.7 32.4 %collective-permute-start.11 = (bf16[2,384,384]{2,1,0:T(8,128)(2,1)S(1)}, bf16[2,384,384]{2,1,0:T(8,128)(2,1)}, u32[]{:S(2)}, u32[]{:S(2)}) collective-permute-start(bf16[2,384,384]{2,1,0:T(8,128)(2,1)S(1)} %copy-done.22), channel_id=1, source_target_pairs={{0,64},{8,72},{16,80},{24,88},{32,96},{40,104},{48,112},{56,120},{... | collective-permute-start | bytes 1769480 | tf_op jit(solution)/shard_map/ppermute | solution.py:24
  70.5 31.6 %collective-permute-start.9 = (bf16[2,384,384]{2,1,0:T(8,128)(2,1)S(1)}, bf16[2,384,384]{2,1,0:T(8,128)(2,1)}, u32[]{:S(2)}, u32[]{:S(2)}) collective-permute-start(bf16[2,384,384]{2,1,0:T(8,128)(2,1)S(1)} %copy-done.22), channel_id=1, source_target_pairs={{0,32},{8,40},{16,48},{24,56},{32,64},{40,72},{48,80},{56,88},{64,... | collective-permute-start | bytes 1769480 | tf_op jit(solution)/shard_map/ppermute | solution.py:24
  95.3 69.6 %collective-permute-start.21 = (bf16[8,192,640]{2,1,0:T(8,128)(2,1)S(1)}, bf16[8,192,640]{2,1,0:T(8,128)(2,1)}, u32[]{:S(2)}, u32[]{:S(2)}) collective-permute-start(bf16[8,192,640]{2,1,0:T(8,128)(2,1)S(1)} %all-to-all-done), channel_id=1, source_target_pairs={{0,8},{8,0},{16,24},{24,16},{32,40},{40,32},{48,56},{56,48},{64,72... | collective-permute-start | bytes 5898248 | tf_op jit(solution)/shard_map/ppermute | solution.py:24
  126.5 18.0 %collective-permute-start.13 = (bf16[384,512]{1,0:T(8,128)(2,1)}, bf16[384,512]{1,0:T(8,128)(2,1)S(1)}, u32[]{:S(2)}, u32[]{:S(2)}) collective-permute-start(bf16[384,512]{1,0:T(8,128)(2,1)} %get-tuple-element.27), channel_id=1, source_target_pairs={{0,16},{8,24},{16,0},{24,8},{32,48},{40,56},{48,32},{56,40},{64,80... | collective-permute-start | bytes 1179656 | tf_op jit(solution)/shard_map/ppermute | solution.py:24
  154.1 15.7 %collective-permute-start.15 = (bf16[384,384]{1,0:T(8,128)(2,1)}, bf16[384,384]{1,0:T(8,128)(2,1)S(1)}, u32[]{:S(2)}, u32[]{:S(2)}) collective-permute-start(bf16[384,384]{1,0:T(8,128)(2,1)} %finish.2.refs_0_), channel_id=1, source_target_pairs={{0,2},{1,3},{2,4},{3,5},{4,6},{5,7},{6,0},{7,1},{8,10},{9,11},{10,... | collective-permute-start | bytes 884744 | tf_op jit(solution)/shard_map/ppermute | solution.py:20
  154.1 15.7 %collective-permute-start.16 = (bf16[384,384]{1,0:T(8,128)(2,1)}, bf16[384,384]{1,0:T(8,128)(2,1)S(1)}, u32[]{:S(2)}, u32[]{:S(2)}) collective-permute-start(bf16[384,384]{1,0:T(8,128)(2,1)} %finish.2.refs_0_), channel_id=1, source_target_pairs={{0,6},{1,7},{2,0},{3,1},{4,2},{5,3},{6,4},{7,5},{8,14},{9,15},{10,... | collective-permute-start | bytes 884744 | tf_op jit(solution)/shard_map/ppermute | solution.py:20
  158.4 15.6 %collective-permute-start.18 = (bf16[384,384]{1,0:T(8,128)(2,1)S(1)}, bf16[384,384]{1,0:T(8,128)(2,1)S(1)}, u32[]{:S(2)}, u32[]{:S(2)}) collective-permute-start(bf16[384,384]{1,0:T(8,128)(2,1)S(1)} %collective-permute-done.14.refs_1_), channel_id=1, source_target_pairs={{0,2},{1,3},{2,4},{3,5},{4,6},{5,7},{6,0},{7,1},{8,10},{9,11},{10,... | collective-permute-start | bytes 884744 | tf_op jit(solution)/shard_map/ppermute | solution.py:20
  181.8 14.8 %collective-permute-start.22 = (bf16[384,640]{1,0:T(8,128)(2,1)}, bf16[384,640]{1,0:T(8,128)(2,1)S(1)}, u32[]{:S(2)}, u32[]{:S(2)}) collective-permute-start(bf16[384,640]{1,0:T(8,128)(2,1)} %add_branch.2.refs_0_.refs_9_), channel_id=1, source_target_pairs={{0,1},{1,0},{2,3},{3,2},{4,5},{5,4},{6,7},{7,6},{8,9},{9,8},{10,11... | collective-permute-start | bytes 1474568 | tf_op jit(solution)/shard_map/ppermute | solution.py:20
  182.1 17.8 %collective-permute-start.25 = (bf16[384,640]{1,0:T(8,128)(2,1)}, bf16[384,640]{1,0:T(8,128)(2,1)S(1)}, u32[]{:S(2)}, u32[]{:S(2)}) collective-permute-start(bf16[384,640]{1,0:T(8,128)(2,1)} %add_branch.2.refs_0_.refs_9_), channel_id=1, source_target_pairs={{0,4},{1,5},{2,6},{3,7},{4,0},{5,1},{6,2},{7,3},{8,12},{9,13},{10,... | collective-permute-start | bytes 1474568 | tf_op jit(solution)/shard_map/ppermute | solution.py:20
  183.9 23.4 %collective-permute-start.23 = (bf16[384,640]{1,0:T(8,128)(2,1)}, bf16[384,640]{1,0:T(8,128)(2,1)S(1)}, u32[]{:S(2)}, u32[]{:S(2)}) collective-permute-start(bf16[384,640]{1,0:T(8,128)(2,1)} %add_branch.2.refs_0_.refs_9_), channel_id=1, source_target_pairs={{0,2},{1,3},{2,4},{3,5},{4,6},{5,7},{6,0},{7,1},{8,10},{9,11},{10,... | collective-permute-start | bytes 1474568 | tf_op jit(solution)/shard_map/ppermute | solution.py:20
  185.3 22.9 %collective-permute-start.24 = (bf16[384,640]{1,0:T(8,128)(2,1)}, bf16[384,640]{1,0:T(8,128)(2,1)S(1)}, u32[]{:S(2)}, u32[]{:S(2)}) collective-permute-start(bf16[384,640]{1,0:T(8,128)(2,1)} %add_branch.2.refs_0_.refs_9_), channel_id=1, source_target_pairs={{0,6},{1,7},{2,0},{3,1},{4,2},{5,3},{6,4},{7,5},{8,14},{9,15},{10,... | collective-permute-start | bytes 1474568 | tf_op jit(solution)/shard_map/ppermute | solution.py:20
  196.7 21.1 %collective-permute-start.26 = (bf16[384,640]{1,0:T(8,128)(2,1)S(1)}, bf16[384,640]{1,0:T(8,128)(2,1)S(1)}, u32[]{:S(2)}, u32[]{:S(2)}) collective-permute-start(bf16[384,640]{1,0:T(8,128)(2,1)S(1)} %collective-permute-done.22.refs_1_), channel_id=1, source_target_pairs={{0,2},{1,3},{2,4},{3,5},{4,6},{5,7},{6,0},{7,1},{8,10},{9,11},{10,... | collective-permute-start | bytes 1474568 | tf_op jit(solution)/shard_map/ppermute | solution.py:20
  197.3 20.4 %collective-permute-start.27 = (bf16[384,640]{1,0:T(8,128)(2,1)S(1)}, bf16[384,640]{1,0:T(8,128)(2,1)S(1)}, u32[]{:S(2)}, u32[]{:S(2)}) collective-permute-start(bf16[384,640]{1,0:T(8,128)(2,1)S(1)} %collective-permute-done.22.refs_1_), channel_id=1, source_target_pairs={{0,6},{1,7},{2,0},{3,1},{4,2},{5,3},{6,4},{7,5},{8,14},{9,15},{10,... | collective-permute-start | bytes 1474568 | tf_op jit(solution)/shard_map/ppermute | solution.py:20
  199.9 17.8 %collective-permute-start.28 = (bf16[384,640]{1,0:T(8,128)(2,1)S(1)}, bf16[384,640]{1,0:T(8,128)(2,1)S(1)}, u32[]{:S(2)}, u32[]{:S(2)}) collective-permute-start(bf16[384,640]{1,0:T(8,128)(2,1)S(1)} %collective-permute-done.25.refs_4_), channel_id=1, source_target_pairs={{0,1},{1,0},{2,3},{3,2},{4,5},{5,4},{6,7},{7,6},{8,9},{9,8},{10,11... | collective-permute-start | bytes 1474568 | tf_op jit(solution)/shard_map/ppermute | solution.py:20
  239.4 29.0 %collective-permute-start.31 = (bf16[2,384,384]{2,1,0:T(8,128)(2,1)}, bf16[2,384,384]{2,1,0:T(8,128)(2,1)S(1)}, u32[]{:S(2)}, u32[]{:S(2)}) collective-permute-start(bf16[2,384,384]{2,1,0:T(8,128)(2,1)} %get-tuple-element.31.refs_0_.refs_1_), channel_id=1, source_target_pairs={{0,32},{8,40},{16,48},{24,56},{32,64},{40,72},{48,80},{56,88},{64,... | collective-permute-start | bytes 1769480 | tf_op jit(solution)/shard_map/ppermute | solution.py:24
  239.4 29.0 %collective-permute-start.32 = (bf16[2,384,384]{2,1,0:T(8,128)(2,1)}, bf16[2,384,384]{2,1,0:T(8,128)(2,1)S(1)}, u32[]{:S(2)}, u32[]{:S(2)}) collective-permute-start(bf16[2,384,384]{2,1,0:T(8,128)(2,1)} %get-tuple-element.31.refs_0_.refs_1_), channel_id=1, source_target_pairs={{0,96},{8,104},{16,112},{24,120},{32,0},{40,8},{48,16},{56,24},{64... | collective-permute-start | bytes 1769480 | tf_op jit(solution)/shard_map/ppermute | solution.py:24
  242.7 25.8 %collective-permute-start.33 = (bf16[2,384,384]{2,1,0:T(8,128)(2,1)}, bf16[2,384,384]{2,1,0:T(8,128)(2,1)S(1)}, u32[]{:S(2)}, u32[]{:S(2)}) collective-permute-start(bf16[2,384,384]{2,1,0:T(8,128)(2,1)} %get-tuple-element.31.refs_0_.refs_1_), channel_id=1, source_target_pairs={{0,64},{8,72},{16,80},{24,88},{32,96},{40,104},{48,112},{56,120},{... | collective-permute-start | bytes 1769480 | tf_op jit(solution)/shard_map/ppermute | solution.py:24
  247.6 21.0 %collective-permute-start.30 = (bf16[768,384]{1,0:T(8,128)(2,1)S(1)}, bf16[768,384]{1,0:T(8,128)(2,1)S(1)}, u32[]{:S(2)}, u32[]{:S(2)}) collective-permute-start(bf16[768,384]{1,0:T(8,128)(2,1)S(1)} %constant_dynamic-update-slice_fusion.2.qa_ref), channel_id=1, source_target_pairs={{0,8},{8,0},{16,24},{24,16},{32,40},{40,32},{48,56},{56,48},{64,72... | collective-permute-start | bytes 1769480 | tf_op jit(solution)/shard_map/ppermute | solution.py:24
  293.3 18.3 %collective-permute-start.35 = (bf16[384,512]{1,0:T(8,128)(2,1)}, bf16[384,512]{1,0:T(8,128)(2,1)S(1)}, u32[]{:S(2)}, u32[]{:S(2)}) collective-permute-start(bf16[384,512]{1,0:T(8,128)(2,1)} %get-tuple-element.37), channel_id=1, source_target_pairs={{0,16},{8,24},{16,0},{24,8},{32,48},{40,56},{48,32},{56,40},{64,80... | collective-permute-start | bytes 1179656 | tf_op jit(solution)/shard_map/ppermute | solution.py:24
  318.4 15.8 %collective-permute-start.37 = (bf16[384,384]{1,0:T(8,128)(2,1)}, bf16[384,384]{1,0:T(8,128)(2,1)S(1)}, u32[]{:S(2)}, u32[]{:S(2)}) collective-permute-start(bf16[384,384]{1,0:T(8,128)(2,1)} %finish.3.refs_0_), channel_id=1, source_target_pairs={{0,2},{1,3},{2,4},{3,5},{4,6},{5,7},{6,0},{7,1},{8,10},{9,11},{10,... | collective-permute-start | bytes 884744 | tf_op jit(solution)/shard_map/ppermute | solution.py:20
  324.9 15.6 %collective-permute-start.40 = (bf16[384,384]{1,0:T(8,128)(2,1)S(1)}, bf16[384,384]{1,0:T(8,128)(2,1)S(1)}, u32[]{:S(2)}, u32[]{:S(2)}) collective-permute-start(bf16[384,384]{1,0:T(8,128)(2,1)S(1)} %collective-permute-done.36.refs_1_), channel_id=1, source_target_pairs={{0,2},{1,3},{2,4},{3,5},{4,6},{5,7},{6,0},{7,1},{8,10},{9,11},{10,... | collective-permute-start | bytes 884744 | tf_op jit(solution)/shard_map/ppermute | solution.py:20
  325.6 14.8 %collective-permute-start.41 = (bf16[384,384]{1,0:T(8,128)(2,1)S(1)}, bf16[384,384]{1,0:T(8,128)(2,1)S(1)}, u32[]{:S(2)}, u32[]{:S(2)}) collective-permute-start(bf16[384,384]{1,0:T(8,128)(2,1)S(1)} %collective-permute-done.36.refs_1_), channel_id=1, source_target_pairs={{0,6},{1,7},{2,0},{3,1},{4,2},{5,3},{6,4},{7,5},{8,14},{9,15},{10,... | collective-permute-start | bytes 884744 | tf_op jit(solution)/shard_map/ppermute | solution.py:20
  (54 other events, 358.0 us)
